TPU v7x, 128 devices: a whole 4x4x4 slice. The times are simulated.
128 devices in a mesh: depth: 8 (over y_lo, z), rows: 2 (over core), cols: 8 (over x, y_hi).
Axes of the slice: x: 4, y: 4 (y_hi: 2, y_lo: 2; y = y_hi * 2 + y_lo), z: 4, core: 2. Of those that a mesh axis runs over, the one named last changes fastest.
Arguments:
- lower_panels: bfloat16 [16, 8, 768, 1024], P('depth', None, None, ('rows', 'cols')), may hold values from -0.23925781 to 0.23925781
- upper_panels: bfloat16 [16, 1024, 6144], P('depth', 'rows', 'cols'), may hold values from -0.23925781 to 0.23925781
- given_inverse: bfloat16 [16, 1024, 1024], P('depth', 'rows'), may hold values from -0.05625 to 2, as said below
- structure: int32 [16, 48], P('depth'), may hold values 0 or 1
- ancestor_entries: float32 [6144, 6144], P(('depth', 'rows'), 'cols'), may hold values from -0.6 to 19.2, as said below
Outputs:
- column_factor: float32 [6144, 512], P(('depth', 'rows'))
- trailing: float32 [6144, 6144], P(('depth', 'rows'), 'cols')
Inputs may be any that keep to these rules, and one draw needn't show every extreme that they name: `given_inverse`: off-diagonal entries are small against the diagonal. `ancestor_entries`: diagonal entries lie between 12.8 and 19.2.
All inputs are finite; a program needn't handle non-finite values. No bound on the sum of `structure` on one device may be relied on, other than what follows from the above.
Results may differ from a plain program's by a relative error of at most 0.0003.
Values may be sent and summed in bfloat16 or wider, within the bound.
A program may use at most 128 MiB of HBM per device.

v0:
```python
import jax
import jax.numpy as jnp
from jax import lax
from jax.sharding import PartitionSpec as P

PW = 512
NEWTON = 2


def from_root(array, axis, root):
    mine = lax.axis_index(axis) == root
    return lax.psum(jnp.where(mine, array, jnp.zeros_like(array)), axis)


def local(lower_panels, upper_panels, given_inverse, structure, ancestor_entries):
    highest = lax.Precision.HIGHEST
    subtree_count = lower_panels.shape[0]
    depth_count = lax.axis_size("depth")
    rows_count = lax.axis_size("rows")
    block_rows = lower_panels.shape[2]
    local_cols = upper_panels.shape[2]
    row_share = block_rows // rows_count
    block_count = structure.shape[1]
    block_size = depth_count * block_rows // block_count
    kept_blocks = (structure != 0).astype(jnp.bfloat16)
    lower_masked = (
        lower_panels.reshape(subtree_count, block_count, block_size, lower_panels.shape[3])
        * kept_blocks[:, :, None, None]
    ).reshape(lower_panels.shape)
    col_blocks = local_cols // block_size
    col_kept = lax.dynamic_slice_in_dim(
        kept_blocks, lax.axis_index("cols") * col_blocks, col_blocks, 1
    )
    upper_masked = (
        upper_panels.reshape(subtree_count, upper_panels.shape[1], col_blocks, block_size)
        * col_kept[:, None, :, None]
    ).reshape(upper_panels.shape)
    upper_full = lax.all_gather(upper_masked, "rows", axis=1, tiled=True)
    applied_half = jnp.einsum(
        "sik,skc->sic", given_inverse, upper_full, preferred_element_type=jnp.float32
    ).astype(jnp.bfloat16)
    update = jnp.einsum(
        "sjqk,skc->jqc",
        lax.all_gather(lower_masked, "cols", axis=3, tiled=True),
        applied_half,
        preferred_element_type=jnp.float32,
    )
    negated = (-update).reshape(depth_count * rows_count, row_share, local_cols)
    owned_sum = lax.psum_scatter(negated, ("depth", "rows"), scatter_dimension=0, tiled=True)[0]
    ancestor = ancestor_entries + owned_sum
    first_row = lax.axis_index(("depth", "rows")) * row_share
    row_offset = jnp.arange(PW, dtype=jnp.int32) - first_row
    inside = (row_offset >= 0) & (row_offset < row_share)
    picked = jnp.take(ancestor, jnp.clip(row_offset, 0, row_share - 1), axis=0)
    picked = jnp.where(inside[:, None], picked, jnp.zeros_like(picked))
    top_block = lax.psum(picked, ("depth", "rows"))
    column_panel, pivot = (
        from_root(ancestor[:, :PW], "cols", 0),
        from_root(top_block[:, :PW], "cols", 0),
    )
    identity = jnp.eye(PW, dtype=jnp.float32)
    inverse = identity / 16.0
    for sweep in range(NEWTON):
        product = jnp.dot(pivot, inverse, precision=highest)
        inverse = jnp.dot(inverse, 2.0 * identity - product, precision=highest)
    column_factor = jnp.dot(column_panel, inverse, precision=highest)
    trailing = ancestor - jnp.dot(column_factor, top_block, precision=highest)
    return (column_factor, trailing)


def solution(mesh):
    return jax.shard_map(
        local,
        mesh=mesh,
        in_specs=(
            P("depth", None, None, ("rows", "cols")),
            P("depth", "rows", "cols"),
            P("depth", "rows", None),
            P("depth", None),
            P(("depth", "rows"), "cols"),
        ),
        out_specs=(P(("depth", "rows"), None), P(("depth", "rows"), "cols")),
        check_vma=False,
    )
```

profile of v0, /device:TPU:111, one launch (start us, length us, event | category | flops | bytes accessed | tf_op | source)
XLA Modules:
  0.0 556.9 jit_solution(16396072703336000724)
XLA Ops:
  7.2 0.0 copy-start
  7.2 0.0 all-gather.5.cloned.1.call-start
  7.2 0.8 compare_convert_fusion
  8.1 0.1 constant_dynamic-slice_fusion
  8.1 0.1 broadcast_bitcast_fusion
  8.2 2.7 broadcast_multiply_fusion
  10.9 0.0 all-gather.5.cloned.1.call-update
  10.9 0.0 all-gather.3.cloned.1.call-start
  11.0 0.1 mul.41
  11.0 0.1 mul.42
  11.1 2.7 copy_multiply_fusion
  13.8 0.0 all-gather.3.cloned.1.call-update
  13.8 0.0 reduce-scatter.2.cloned.1.call-start
  13.9 13.7 %all-gather.5.cloned.1.call-done = bf16[2,1024,768]{2,1,0:T(8,128)(2,1)} async-done(((bf16[2,512,768]{2,1,0:T(8,128)(2,1)}), bf16[2,1024,768]{2,1,0:T(8,128)(2,1)}) %all-gather.5.cloned.1.call-update) | async-done | bytes 3145744 | tf_op jit(solution)/shard_map/all_gather | solution.py:38
  27.6 147.4 %all-gather.3.cloned.1.call-done = bf16[2,8,768,512]{2,3,0,1:T(8,128)(2,1)} async-done(((bf16[2,8,768,64]{2,3,0,1:T(8,128)(2,1)}), bf16[2,8,768,512]{2,3,0,1:T(8,128)(2,1)}) %all-gather.3.cloned.1.call-update) | async-done | bytes 12582928 | tf_op jit(solution)/shard_map/all_gather | solution.py:44
  174.9 0.0 copy-done
  174.9 20.8 %bitcast_negate_fusion = f32[8,768,768]{2,1,0:T(8,128)} fusion(bf16[2,8,768,512]{2,3,0,1:T(8,128)(2,1)} %all-gather.3.cloned.1.call-done, bf16[2,512,1024]{2,1,0:T(8,128)(2,1)S(1)} %copy-done, bf16[2,1024,768]{2,1,0:T(8,128)(2,1)} %all-gather.5.cloned.1.call-done), kind=kOutput, calls=%fused_computation.1 | convolution fusion | flops 11279794176 | bytes 36700160 | tf_op jit(solution)/shard_map/sjqk,skc->jqc/dot_general | solution.py:42
  195.7 0.0 reduce-scatter.2.cloned.1.call-update
  195.7 0.0 all-reduce.4.cloned.1.call-start
  195.8 107.8 %reduce-scatter.2.cloned.1.call-done = f32[1,384,768]{2,1,0:T(8,128)} async-done(((f32[16,384,768]{2,1,0:T(8,128)}), f32[1,384,768]{2,1,0:T(8,128)}) %reduce-scatter.2.cloned.1.call-update) | async-done | bytes 1179664 | tf_op jit(solution)/shard_map/reduce_scatter | solution.py:49
  303.7 1.8 bitcast_add_fusion
  305.4 2.6 gather_fusion
  308.0 2.8 select_select_fusion
  310.8 0.0 all-reduce.4.cloned.1.call-update
  310.8 0.2 all-reduce.6.cloned.1.call-start
  311.1 1.0 slice_select_fusion.1
  312.1 121.7 %all-reduce.4.cloned.1.call-done = f32[512,768]{1,0:T(8,128)} async-done(((f32[512,768]{1,0:T(8,128)}), f32[512,768]{1,0:T(8,128)}) %all-reduce.4.cloned.1.call-update) | async-done | bytes 1572880 | tf_op jit(solution)/shard_map/psum | solution.py:56
  433.8 2.3 slice_select_fusion
  436.1 0.0 all-reduce.6.cloned.1.call-update
  436.1 101.1 %all-reduce.6.cloned.1.call-done = (f32[384,512]{1,0:T(8,128)}, f32[512,512]{1,0:T(8,128)}) async-done(((f32[384,512]{1,0:T(8,128)}, f32[512,512]{1,0:T(8,128)}), (f32[384,512]{1,0:T(8,128)}, f32[512,512]{1,0:T(8,128)})) %all-reduce.6.cloned.1.call-update) | async-done | bytes 1835024 | tf_op jit(solution)/shard_map/psum | solution.py:12
  537.2 3.0 select_subtract_fusion.1
  540.2 0.0 copy-start.3
  540.2 1.8 fusion.1
  542.0 0.0 copy-done.3
  542.0 1.8 select_subtract_fusion
  543.9 0.0 copy-start.4
  543.9 1.9 fusion.18
  545.8 0.0 copy-start.1
  545.8 0.0 copy-done.4
  545.8 1.4 fusion.19
  547.2 0.0 copy-done.1
  547.2 0.0 copy-start.2
  547.3 3.1 convolution_subtract_fusion
  550.4 0.0 copy-done.2
  (5 shorter events, 0.1 us)
Async XLA Ops:
  7.2 167.8 %copy-start = (bf16[2,512,1024]{2,1,0:T(8,128)(2,1)S(1)}, bf16[2,512,1024]{2,1,0:T(8,128)(2,1)}, u32[]{:S(2)}) copy-start(bf16[2,512,1024]{2,1,0:T(8,128)(2,1)} %param.7) | copy-start | bytes 6291460
  7.2 20.4 %all-gather.5.cloned.1.call-start = ((), (), s32[]{:S(2)}) async-start(), calls=%async_computation.2 | async-start | bytes 4718592 | tf_op jit(solution)/shard_map/all_gather | solution.py:38
  10.9 164.0 %all-gather.3.cloned.1.call-start = ((), (), s32[]{:S(2)}) async-start(), calls=%async_computation.1 | async-start | bytes 14155776 | tf_op jit(solution)/shard_map/all_gather | solution.py:44
  13.8 289.8 %reduce-scatter.2.cloned.1.call-start = ((), (), s32[]{:S(2)}) async-start(), calls=%async_computation.3 | async-start | bytes 20054016 | tf_op jit(solution)/shard_map/reduce_scatter | solution.py:49
  195.7 238.1 %all-reduce.4.cloned.1.call-start = ((), (), s32[]{:S(2)}) async-start(), calls=%async_computation.4 | async-start | bytes 3145728 | tf_op jit(solution)/shard_map/psum | solution.py:56
  310.8 226.4 %all-reduce.6.cloned.1.call-start = ((), (), s32[]{:S(2)}) async-start(), calls=%async_computation.5 | async-start | bytes 3670016 | tf_op jit(solution)/shard_map/psum | solution.py:12
  540.2 1.8 copy-start.3
  543.9 1.9 copy-start.4
  545.8 1.5 copy-start.1
  547.2 3.1 copy-start.2
Sparse Core Ops, SparseCore 0:
  11.0 16.4 all-gather.4
  29.9 144.9 all-gather.2
  195.9 107.7 reduce-scatter.1
  311.0 122.7 all-reduce.3
  437.0 100.1 all-reduce.5
where the time goes:
time: 563 us; the launch traced here: 557 us
  waiting for transfers between devices  492 us (87%)
  matrix products  33.9 us (6%)
  other arithmetic  14 us (2%)
  between operations  13.9 us (2%)
    all_gather x1, waiting for transfers between devices, local(): lax.all_gather(lower_masked, 'cols', axis=3, tiled=True)  147 us
    psum x1, waiting for transfers between devices, local(): top_block = lax.psum(picked, ('depth', 'rows'))  122 us
    reduce_scatter x1, waiting for transfers between devices, local(): lax.psum_scatter(negated, ('depth', 'rows'), scatter_dimension=0, tiled=T...  108 us
    psum x1, waiting for transfers between devices, from_root(): return lax.psum(jnp.where(mine, array, jnp.zeros_like(array)), axis)  101 us
    dot_general x1, matrix products, local(): jnp.einsum('sjqk,skc->jqc', lax.all_gather(lower_masked, 'cols', axis=3,...  20.8 us
    all_gather x1, waiting for transfers between devices, local(): upper_full = lax.all_gather(upper_masked, 'rows', axis=1, tiled=True)  13.7 us
  transfers between devices with their start and end apart: 5, of which 5 were waited for; matrix products, arithmetic and copies ran while one was open for 1% of the time, Pallas kernels for 0%

commit v1 on v0

v1 whole, which is shorter than its diff:
```python
import functools

import jax
import jax.numpy as jnp
from jax import lax
from jax.experimental import pallas as pl
from jax.experimental.pallas import tpu as pltpu
from jax.sharding import PartitionSpec as P

PW = 512
BLOCK = 128
MESH = pl.DeviceIdType.MESH
VMEM = pl.BlockSpec(memory_space=pltpu.VMEM)
LIMIT = 56 * 1024 * 1024
OFFSETS = (2, 1, 3, 0)
TOP = 32000.0


def place():
    depth, rows, cols = lax.axis_index("depth"), lax.axis_index("rows"), lax.axis_index("cols")
    return depth // 4, depth % 4, rows, cols // 2, cols % 2


def device(low, z, core, x, half):
    return (low * 4 + z, core, x * 2 + half)


def quantize(value):
    most = jnp.maximum(jnp.max(jnp.abs(value), axis=0, keepdims=True), 1e-30)
    return jnp.round(value * (TOP / most)).astype(jnp.int16), most / TOP


def update_kernel(
    low_ref, up_ref, inv_ref, mask_ref, ent_ref, out_ref,
    up_other, app, lg, cq, cs, rq, rs, own, sq, ss, tq, ts,
    up_sem, l1_sem, loc_sem, l2_sem, f_sem, core_sem, half_sem, fwd_sem,
    r1_sem, r1s_sem, r2_sem, r2s_sem,
):
    low, z, core, x, half = place()

    def remote(src, dst, sems, index, target):
        return pltpu.make_async_remote_copy(
            src_ref=src, dst_ref=dst, send_sem=sems.at[0, index], recv_sem=sems.at[1, index],
            device_id=target, device_id_type=MESH,
        )

    partner = device(low, z, 1 - core, x, half)
    across = device(low, z, core, x, 1 - half)
    across_core = device(low, z, 1 - core, x, 1 - half)
    right = device(low, z, core, (x + 1) % 4, half)
    left = device(low, z, core, (x + 3) % 4, half)
    along_z = {o: device(low, (z + o) % 4, core, x, half) for o in (1, 2, 3)}
    along_y = [
        across,
        device(1 - low, z, core, x, half),
        device(1 - low, z, core, x, 1 - half),
    ]

    barrier = pltpu.get_barrier_semaphore()
    friends = [partner, across, across_core, right, left, *along_z.values(), *along_y[1:]]
    for friend in friends:
        pl.semaphore_signal(barrier, inc=1, device_id=friend, device_id_type=MESH)
    pl.semaphore_wait(barrier, len(friends))

    upper_copy = remote(up_ref, up_other, up_sem, 0, partner)
    upper_copy.start()

    lane = pl.multiple_of((x * 4 + core * 2 + half) * 128, 128)
    stage1, kept = [], []
    for q, o in enumerate(OFFSETS):
        owner = (z + o) % 4
        here = pltpu.make_async_copy(
            low_ref.at[owner, core, half], lg.at[q, :, pl.ds(lane, 128)], loc_sem.at[q]
        )
        here.start()
        kept.append(here)
        sends = []
        for t, (target, r, h) in enumerate((
            (across, core, 1 - half), (across_core, 1 - core, 1 - half), (partner, 1 - core, half),
        )):
            copy = remote(
                low_ref.at[owner, r, h], lg.at[q, :, pl.ds(lane, 128)], l1_sem, q * 3 + t, target
            )
            copy.start()
            sends.append(copy)
        stage1.append(sends)

    upper_copy.wait()
    mine, theirs = pl.multiple_of(core * 512, 512), pl.multiple_of((1 - core) * 512, 512)
    for s in range(2):

        @pl.loop(0, 3)
        def _(tile):
            cols = pl.ds(pl.multiple_of(tile * 256, 256), 256)
            total = jnp.dot(
                inv_ref[s, :, pl.ds(mine, 512)], up_ref[s, :, cols], preferred_element_type=jnp.float32
            ) + jnp.dot(
                inv_ref[s, :, pl.ds(theirs, 512)], up_other[s, :, cols], preferred_element_type=jnp.float32
            )
            applied = (total * mask_ref[s:s + 1, cols]).astype(jnp.bfloat16)
            for c in range(8):
                app[half, c // 2, core, (c % 2) * 128 + s * 64:(c % 2) * 128 + s * 64 + 64, cols] = (
                    applied[c * 64:(c + 1) * 64]
                )

    core_copy = remote(app.at[half, :, core], app.at[half, :, core], core_sem, 0, partner)
    core_copy.start()
    half_copies = []
    for p in range(2):
        part = app.at[half, pl.ds(p * 2, 2), core]
        copy = remote(part, part, half_sem, p, across)
        copy.start()
        half_copies.append(copy)

    def ring(q):
        kept[q].wait()
        for copy in stage1[q]:
            copy.wait_recv()
        block = lg.at[q, :, pl.ds(pl.multiple_of(x * 512, 512), 512)]
        copies = [remote(block, block, l2_sem, q * 2, right), remote(block, block, l2_sem, q * 2 + 1, left)]
        for copy in copies:
            copy.start()
        return copies

    def forward(q):
        from_left = pl.multiple_of(((x + 3) % 4) * 512, 512)
        from_right = pl.multiple_of(((x + 1) % 4) * 512, 512)
        first = lg.at[q, pl.ds(0, 192), pl.ds(from_left, 512)]
        second = lg.at[q, pl.ds(192, 192), pl.ds(from_right, 512)]
        copies = [remote(first, first, f_sem, q * 2, right), remote(second, second, f_sem, q * 2 + 1, left)]
        for copy in copies:
            copy.start()
        return copies

    def contribute(q, side):
        o = OFFSETS[q]

        @pl.loop(0, 3)
        def _(tile):
            cols = pl.ds(pl.multiple_of(tile * 256, 256), 256)
            total = jnp.dot(
                lg[q], app[side, :, :, :, cols].reshape(2048, 256), preferred_element_type=jnp.float32
            )
            if o == 0:
                own[side, :, cols] = total
            else:
                values, scale = quantize(total)
                cq[o - 1, side, :, cols] = values
                cs[o - 1, side, :, cols] = jnp.broadcast_to(scale, (8, 256))

        if o == 0:
            return []
        turn = (o - 1) * 2
        return [
            (cq.at[o - 1, side], rq.at[o - 1, side], r1_sem, turn, along_z[o]),
            (cs.at[o - 1, side], rs.at[o - 1, side], r1s_sem, turn, along_z[o]),
        ]

    sent = []

    def give(q, own_side):
        side = half if own_side else 1 - half
        for src, dst, sems, turn, target in contribute(q, side):
            copy = remote(src, dst, sems, turn + (0 if own_side else 1), target)
            copy.start()
            sent.append(copy)

    stage2, passed = {}, {}
    stage2[0] = ring(0)
    core_copy.wait_recv()
    for q in range(4):
        for copy in stage2[q]:
            copy.wait_recv()
        passed[q] = forward(q)
        if q < 3:
            stage2[q + 1] = ring(q + 1)
        if q > 0:
            for copy in passed[q - 1]:
                copy.wait_recv()
            give(q - 1, True)
    forwards = []
    for p, copy in enumerate(half_copies):
        copy.wait_recv()
        part = app.at[1 - half, pl.ds(p * 2, 2), core]
        onward = remote(part, part, fwd_sem, p, partner)
        onward.start()
        forwards.append(onward)
    for copy in forwards:
        copy.wait_recv()
    for q in range(3):
        give(q, False)
    for copy in passed[3]:
        copy.wait_recv()
    give(3, True)
    give(3, False)

    for copy in sent:
        copy.wait_recv()
    moved = []
    here = None
    for t, (row, col) in enumerate((
        (low, 1 - half), (1 - low, half), (1 - low, 1 - half), (low, half),
    )):
        rows = pl.ds(pl.multiple_of(row * 192, 192), 192)
        total = own[col, rows, :]
        for o in range(3):
            total = total + rq[o, col, rows, :].astype(jnp.float32) * rs[o, col, 0:1, :]
        if t < 3:
            values, scale = quantize(total)
            sq[t] = values
            ss[t] = jnp.broadcast_to(scale, (8, 768))
            for copy in (
                remote(sq.at[t], tq.at[t], r2_sem, t, along_y[t]),
                remote(ss.at[t], ts.at[t], r2s_sem, t, along_y[t]),
            ):
                copy.start()
                moved.append(copy)
        else:
            own[col, rows, :] = total
    for copy in moved:
        copy.wait_recv()

    def arrived(t):
        return tq[t].astype(jnp.float32) * ts[t, 0:1, :]

    mine = pl.ds(pl.multiple_of(half * 192, 192), 192)
    other = pl.ds(pl.multiple_of((1 - half) * 192, 192), 192)
    kept_rows = pl.ds(pl.multiple_of(low * 192, 192), 192)
    out_ref[mine, :] = ent_ref[mine, :] - (own[half, kept_rows, :] + arrived(1))
    out_ref[other, :] = ent_ref[other, :] - (arrived(0) + arrived(2))

    upper_sends = [c for sends in stage1 for c in sends]
    for group in (upper_sends, *stage2.values(), *passed.values(), [core_copy], half_copies, forwards, sent, moved):
        for copy in group:
            copy.wait_send()


def split(value):
    high = value.astype(jnp.bfloat16)
    return high, (value - high.astype(jnp.float32)).astype(jnp.bfloat16)


def dot3(a, b):
    (ah, al), (bh, bl) = split(a), split(b)
    dot = functools.partial(jnp.dot, preferred_element_type=jnp.float32)
    return dot(ah, bh) + (dot(ah, bl) + dot(al, bh))


def panel_kernel(
    anc_ref, cf_ref, out_ref, top, cf, top_sem, tg_sem, core_sem, cf_sem, cg_sem, loc_sem
):
    depth, core, col = lax.axis_index("depth"), lax.axis_index("rows"), lax.axis_index("cols")

    def remote(src, dst, sems, index, target):
        return pltpu.make_async_remote_copy(
            src_ref=src, dst_ref=dst, send_sem=sems.at[0, index], recv_sem=sems.at[1, index],
            device_id=target, device_id_type=MESH,
        )

    barrier = pltpu.get_barrier_semaphore()
    friends = [((depth + o // 2) % 8, core if o % 2 == 0 else 1 - core, col) for o in range(1, 16)]
    friends += [(depth, core, (col + o) % 8) for o in range(1, 8)]
    for friend in friends:
        pl.semaphore_signal(barrier, inc=1, device_id=friend, device_id_type=MESH)
    pl.semaphore_wait(barrier, len(friends))

    def piece_copy(p):
        row = p * 32 - (0 if p < 12 else 384)
        return remote(
            anc_ref.at[pl.ds(row, 32)], top.at[p // 2, p % 2], top_sem, p, (p // 2, p % 2, col)
        )

    first_piece = pltpu.make_async_copy(anc_ref.at[pl.ds(0, 32)], top.at[0, 0], loc_sem)

    @pl.when((depth == 0) & (core == 0))
    def _():
        for p in range(1, 12):
            piece_copy(p).start()
        first_piece.start()
        first_piece.wait()

    @pl.when((depth == 0) & (core == 1))
    def _():
        for p in range(12, 16):
            piece_copy(p).start()

    for p in range(1, 16):

        @pl.when((depth == p // 2) & (core == p % 2))
        def _():
            piece_copy(p).wait_recv()

    gathers = []
    for o in range(1, 8):
        piece = top.at[depth, core]
        copy = remote(piece, piece, tg_sem, o - 1, ((depth + o) % 8, core, col))
        copy.start()
        gathers.append(copy)
    for copy in gathers:
        copy.wait_recv()
    side = top.at[:, core]
    core_copy = remote(side, side, core_sem, 0, (depth, 1 - core, col))
    core_copy.start()
    core_copy.wait_recv()

    def cf_copy(o):
        piece = cf.at[o]
        return remote(piece, piece, cf_sem, o, (depth, core, o))

    def zero_copy(o):
        piece = cf.at[0]
        return remote(piece, piece, cf_sem, 7 + o, (depth, core, o))

    @pl.when(col == 0)
    def _():
        row = lax.broadcasted_iota(jnp.int32, (PW, PW), 0)
        identity = (row == lax.broadcasted_iota(jnp.int32, (PW, PW), 1)).astype(jnp.float32)
        pivot = top[:, :, :, :PW].reshape(PW, PW)
        error = identity - pivot * (1.0 / 16.0)
        square = dot3(error, error)
        inverse = dot3(identity + error, identity + square) * (1.0 / 16.0)
        cf[...] = dot3(anc_ref[:, :PW], inverse).reshape(8, 48, PW)
        for o in range(1, 8):
            cf_copy(o).start()
            zero_copy(o).start()
        for o in range(1, 8):
            cf_copy(o).wait_send()
            zero_copy(o).wait_send()

    def ring_copy(o, target):
        piece = cf.at[col]
        return remote(piece, piece, cg_sem, o - 1, (depth, core, target))

    for c in range(1, 8):

        @pl.when(col == c)
        def _():
            cf_copy(c).wait_recv()
            copies = []
            for o in range(1, 7):
                copy = ring_copy(o, (c - 1 + o) % 7 + 1)
                copy.start()
                copies.append(copy)
            zero_copy(c).wait_recv()
            for copy in copies:
                copy.wait()

    factor = cf[...].reshape(384, PW)
    cf_ref[...] = factor
    fh, fl = split(factor)
    dot = functools.partial(jnp.dot, preferred_element_type=jnp.float32)
    for tile in range(3):
        cols = slice(tile * 256, tile * 256 + 256)
        th, tl = split(top[:, :, :, cols].reshape(PW, 256))
        out_ref[:, cols] = anc_ref[:, cols] - (dot(fh, th) + (dot(fh, tl) + dot(fl, th)))

    for copy in (*gathers, core_copy):
        copy.wait_send()

    @pl.when((depth == 0) & (core == 0))
    def _():
        for p in range(1, 12):
            piece_copy(p).wait_send()

    @pl.when((depth == 0) & (core == 1))
    def _():
        for p in range(12, 16):
            piece_copy(p).wait_send()


def sems(count):
    return pltpu.SemaphoreType.DMA((2, count))


def local(lower_panels, upper_panels, given_inverse, structure, ancestor_entries):
    kept = (structure != 0).astype(jnp.bfloat16)
    kept_rows = jnp.repeat(kept, BLOCK, axis=1)
    lower = lower_panels * kept_rows.reshape(2, 8, 768)[..., None]
    lower = lower.reshape(2, 2, 4, 2, 2, 192, 64).transpose(2, 3, 4, 1, 5, 0, 6).reshape(4, 2, 2, 384, 128)
    col_mask = lax.dynamic_slice_in_dim(kept_rows, lax.axis_index("cols") * 768, 768, 1).astype(jnp.float32)
    f32, bf16, i16 = jnp.float32, jnp.bfloat16, jnp.int16
    ancestor = pl.pallas_call(
        update_kernel,
        name="update",
        out_shape=jax.ShapeDtypeStruct((384, 768), f32),
        in_specs=[VMEM] * 5,
        out_specs=VMEM,
        scratch_shapes=[
            pltpu.VMEM((2, 512, 768), bf16),
            pltpu.VMEM((2, 4, 2, 256, 768), bf16),
            pltpu.VMEM((4, 384, 2048), bf16),
            pltpu.VMEM((3, 2, 384, 768), i16),
            pltpu.VMEM((3, 2, 8, 768), f32),
            pltpu.VMEM((3, 2, 384, 768), i16),
            pltpu.VMEM((3, 2, 8, 768), f32),
            pltpu.VMEM((2, 384, 768), f32),
            pltpu.VMEM((3, 192, 768), i16),
            pltpu.VMEM((3, 8, 768), f32),
            pltpu.VMEM((3, 192, 768), i16),
            pltpu.VMEM((3, 8, 768), f32),
            sems(1), sems(12), pltpu.SemaphoreType.DMA((4,)), sems(8), sems(8), sems(1), sems(2), sems(2),
            sems(6), sems(6), sems(3), sems(3),
        ],
        compiler_params=pltpu.CompilerParams(collective_id=0, has_side_effects=True, vmem_limit_bytes=LIMIT),
    )(lower, upper_panels, given_inverse, col_mask, ancestor_entries)
    return pl.pallas_call(
        panel_kernel,
        name="panel",
        out_shape=(jax.ShapeDtypeStruct((384, PW), f32), jax.ShapeDtypeStruct((384, 768), f32)),
        in_specs=[VMEM],
        out_specs=(VMEM, VMEM),
        scratch_shapes=[
            pltpu.VMEM((8, 2, 32, 768), f32),
            pltpu.VMEM((8, 48, PW), f32),
            sems(16), sems(7), sems(1), sems(15), sems(7), pltpu.SemaphoreType.DMA,
        ],
        compiler_params=pltpu.CompilerParams(collective_id=1, has_side_effects=True, vmem_limit_bytes=LIMIT),
    )(ancestor)


def solution(mesh):
    return jax.shard_map(
        local,
        mesh=mesh,
        in_specs=(
            P("depth", None, None, ("rows", "cols")),
            P("depth", "rows", "cols"),
            P("depth", "rows", None),
            P("depth", None),
            P(("depth", "rows"), "cols"),
        ),
        out_specs=(P(("depth", "rows"), None), P(("depth", "rows"), "cols")),
        check_vma=False,
    )
```

time: 563 us -> 212 us (0.38)
  the two profiles are of different devices: /device:TPU:111 before, /device:TPU:16 now
where the time goes in v1:
time: 212 us
  Pallas kernels  189 us (89%)
  local copies, waits for them, and re-layouts  19 us (9%)
  other arithmetic  3.97 us (2%)
    pallas_call x1, Pallas kernels, local(): pl.pallas_call(update_kernel, name='update', out_shape=jax.ShapeDtypeStru...  129 us
    pallas_call x1, Pallas kernels, local(): pl.pallas_call(panel_kernel, name='panel', out_shape=(jax.ShapeDtypeStruc...  59.1 us
    reshape x4, local copies, waits for them, and re-layouts, local(): lower.reshape(2, 2, 4, 2, 2, 192, 64).transpose(2, 3, 4, 1, 5, 0, 6)  15.6 us

profile of v1, /device:TPU:16, one launch (start us, length us, event | category | flops | bytes accessed | tf_op | source)
XLA Modules:
  0.0 212.2 jit_solution(10343439408139994777)
XLA Ops:
  0.6 0.7 compare_convert_fusion
  1.3 0.1 broadcast_in_dim.3
  1.4 0.1 mul.13
  1.4 2.7 %broadcast_multiply_fusion = bf16[2,8,768,64]{2,3,1,0:T(8,128)(2,1)} fusion(bf16[2,8,768,64]{2,3,1,0:T(8,128)(2,1)} %param.5, bf16[2,8,768]{2,1,0:T(8,128)(2,1)S(1)} %mul.13), kind=kLoop, calls=%fused_computation.1 | loop fusion | flops 786432 | bytes 3170304 | tf_op jit(solution)/shard_map/mul | solution.py:378
  4.1 5.8 %reshape.14 = bf16[2,2,4,2,2,192,64]{5,4,3,6,2,1,0:T(2,128)(2,1)S(1)} reshape(bf16[2,8,768,64]{2,3,1,0:T(8,128)(2,1)} %broadcast_multiply_fusion) | data formatting | bytes 3145728 | tf_op jit(solution)/shard_map/reshape | solution.py:379
  10.0 3.5 %copy.13 = bf16[2,2,4,2,2,192,64]{5,1,6,0,4,3,2:T(2,128)(2,1)} copy(bf16[2,2,4,2,2,192,64]{5,4,3,6,2,1,0:T(2,128)(2,1)S(1)} %reshape.14) | data formatting | bytes 3145728 | tf_op jit(solution)/shard_map/reshape | solution.py:379
  13.5 4.6 %reshape.15 = bf16[4,2,2,384,128]{3,4,2,1,0:T(8,128)(2,1)S(1)} reshape(bf16[4,2,2,2,192,2,64]{4,3,6,5,2,1,0:T(2,128)(2,1)} %bitcast.14) | data formatting | bytes 3145728 | tf_op jit(solution)/shard_map/reshape | solution.py:379
  18.1 1.6 copy.9.low_ref
  19.7 0.1 broadcast_bitcast_fusion
  19.8 0.6 dynamic-slice_convert_fusion.mask_ref
  20.4 129.4 %update.1.anc_ref = f32[384,768]{1,0:T(8,128)} custom-call(bf16[4,2,2,384,128]{4,3,2,1,0:T(8,128)(2,1)} %copy.9.low_ref, bf16[2,512,768]{2,1,0:T(8,128)(2,1)} %up_ref.1, bf16[2,512,1024]{2,1,0:T(8,128)(2,1)} %inv_ref.1, f32[2,768]{1,0:T(2,128)} %dynamic-slice_convert_fusion.mask_ref, f32[384,768]{1,0:T(8,128)} %ent_ref.1), custom_call_target="tpu_custom_call" | custom-call | tf_op jit(solution)/shard_map/update/pallas_call | solution.py:382
  149.9 59.1 %panel.1 = (f32[384,512]{1,0:T(8,128)}, f32[384,768]{1,0:T(8,128)}) custom-call(f32[384,768]{1,0:T(8,128)} %update.1.anc_ref), custom_call_target="tpu_custom_call" | custom-call | tf_op jit(solution)/shard_map/panel/pallas_call | solution.py:406
  209.0 0.0 copy-start
  209.0 2.2 %copy.17 = f32[384,512]{1,0:T(8,128)} copy(f32[384,512]{1,0:T(8,128)} %get-tuple-element.4) | data formatting | bytes 1572864
  211.2 0.0 copy-done
  211.2 1.0 copy.18
  (1 shorter events, 0.0 us)
Async XLA Ops:
  209.0 2.2 %copy-start = (f32[384,768]{1,0:T(8,128)S(1)}, f32[384,768]{1,0:T(8,128)}, u32[]{:S(2)}) copy-start(f32[384,768]{1,0:T(8,128)} %get-tuple-element.5) | copy-start | bytes 3538948

commit v2 on v0

v2 whole, which is shorter than its diff:
```python
import functools

import jax
import jax.numpy as jnp
from jax import lax
from jax.experimental import pallas as pl
from jax.experimental.pallas import tpu as pltpu
from jax.sharding import PartitionSpec as P

PW = 512
MESH = pl.DeviceIdType.MESH
VMEM = pl.BlockSpec(memory_space=pltpu.VMEM)
LIMIT = 58 * 1024 * 1024
OFFSETS = (2, 1, 3, 0)
TOP = 32000.0


def place():
    depth, rows, cols = lax.axis_index("depth"), lax.axis_index("rows"), lax.axis_index("cols")
    return depth // 4, depth % 4, rows, cols // 2, cols % 2


def device(low, z, core, x, half):
    return (low * 4 + z, core, x * 2 + half)


def quantize(value, axis):
    most = jnp.maximum(jnp.max(jnp.abs(value), axis=axis, keepdims=True), 1e-30)
    return jnp.round(value * (TOP / most)).astype(jnp.int16), most / TOP


def split(value):
    high = value.astype(jnp.bfloat16)
    return high, (value - high.astype(jnp.float32)).astype(jnp.bfloat16)


def product(a, b):
    return jnp.dot(a, b, preferred_element_type=jnp.float32)


def dot3(a, b):
    (ah, al), (bh, bl) = split(a), split(b)
    return product(ah, bh) + (product(ah, bl) + product(al, bh))


def received(copies):
    for copy in copies:
        copy.wait_recv()


def whole_kernel(
    kept_ref, low_ref, up_ref, inv_ref, ent_ref, cf_ref, out_ref,
    up_other, turned, turned_top, app, lg, lg_top, cq, cs, rq, rs, own, sq, ss, tq, ts,
    ent_top, ctop, rtop, stop, ttop, top, top_high, top_low, inverse, cf,
    up_sem, l1_sem, loc_sem, l2_sem, f_sem, core_sem, half_sem, fwd_sem,
    r1_sem, r1s_sem, r1b_sem, r1bs_sem, r2_sem, r2s_sem,
    ent_sem, rt_sem, r2t_sem, tg_sem, tc_sem, cf_sem, cg_sem,
):
    low, z, core, x, half = place()
    depth, col = low * 4 + z, x * 2 + half

    def remote(src, dst, sems, index, target):
        return pltpu.make_async_remote_copy(
            src_ref=src, dst_ref=dst, send_sem=sems.at[0, index], recv_sem=sems.at[1, index],
            device_id=target, device_id_type=MESH,
        )

    partner = device(low, z, 1 - core, x, half)
    across = device(low, z, core, x, 1 - half)
    across_core = device(low, z, 1 - core, x, 1 - half)
    right = device(low, z, core, (x + 1) % 4, half)
    left = device(low, z, core, (x + 3) % 4, half)
    along_z = {o: device(low, (z + o) % 4, core, x, half) for o in (1, 2, 3)}
    along_y = [
        across,
        device(1 - low, z, core, x, half),
        device(1 - low, z, core, x, 1 - half),
    ]

    barrier = pltpu.get_barrier_semaphore()
    friends = [((depth + o // 2) % 8, core if o % 2 == 0 else 1 - core, col) for o in range(1, 16)]
    friends += [(depth, core, (col + o) % 8) for o in range(1, 8)]
    friends += [across_core, along_y[2]]
    for friend in friends:
        pl.semaphore_signal(barrier, inc=1, device_id=friend, device_id_type=MESH)
    pl.semaphore_wait(barrier, len(friends))

    upper_copy = remote(up_ref, up_other, up_sem, 0, partner)
    upper_copy.start()

    def entry_copy(g, row):
        target = ((g % 2) * 4 + (g // 2) % 4, g // 16, col)
        return pltpu.make_async_remote_copy(
            src_ref=ent_ref.at[pl.ds(pl.multiple_of(row * 16, 16), 16)], dst_ref=ent_top.at[(g // 8) % 2],
            send_sem=ent_sem.at[0, g], recv_sem=ent_sem.at[1, (g // 8) % 2],
            device_id=target, device_id_type=MESH,
        )

    holder = [(depth == 0) & (core == c) for c in range(2)]
    groups = ([g for g in range(24) if g not in (0, 8)], [g for g in range(25, 32)])
    stays = ([(0, 0), (8, 1)], [(24, 1)])

    def entries(act):
        for c in range(2):

            @pl.when(holder[c])
            def _():
                for g in groups[c]:
                    act(entry_copy(g, g - 24 * c))

    entries(lambda copy: copy.start())
    for c in range(2):

        @pl.when(holder[c])
        def _():
            for g, h in stays[c]:
                row = (g - 24 * c) * 16
                ent_top[h] = ent_ref[row:row + 16, :]

    def factor(s, block):
        return jnp.full((1, 128), kept_ref[s, block].astype(jnp.float32), jnp.float32)

    lane = pl.multiple_of((x * 4 + core * 2 + half) * 128, 128)
    sharers = ((across, core, 1 - half), (across_core, 1 - core, 1 - half), (partner, 1 - core, half))

    def turn_over(j, part):
        lanes = slice(part * 128, part * 128 + 128)
        both = jnp.concatenate(
            [low_ref[s, j, :, lanes] * factor(s, j * 6 + part).astype(jnp.bfloat16) for s in range(2)]
        )
        return both.T

    def share(src, dst, first):
        here = pltpu.make_async_copy(src(core, half), dst, loc_sem.at[first // 3])
        here.start()
        sends = []
        for t, (target, r, h) in enumerate(sharers):
            copy = remote(src(r, h), dst, l1_sem, first + t, target)
            copy.start()
            sends.append(copy)
        return here, sends

    def exchange_top():
        for part in range(4):
            turned_top[part // 2, part % 2] = turn_over(0, part)
        return share(lambda r, h: turned_top.at[r, h], lg_top.at[:, pl.ds(lane, 128)], 24)

    def exchange(q):
        j = (q % 2) * 4 + (z + OFFSETS[q // 2]) % 4
        for part in range(6):
            value = turn_over(j, part)
            for piece in range(2):
                row = part * 128 + piece * 64
                turned[q, row // 384, (row // 192) % 2, row % 192:row % 192 + 64] = (
                    value[piece * 64:piece * 64 + 64]
                )
        return share(lambda r, h: turned.at[q, r, h], lg.at[q, :, pl.ds(lane, 128)], q * 3)

    mine, theirs = pl.multiple_of(core * 512, 512), pl.multiple_of((1 - core) * 512, 512)

    def apply(tile):
        cols = slice(tile * 256, tile * 256 + 256)
        for s in range(2):
            total = product(inv_ref[s, :, pl.ds(mine, 512)], up_ref[s, :, cols]) + product(
                inv_ref[s, :, pl.ds(theirs, 512)], up_other[s, :, cols]
            )
            block = col * 6 + tile * 2
            mask = jnp.concatenate([factor(s, block), factor(s, block + 1)], axis=1)
            applied = (total * mask).astype(jnp.bfloat16)
            for c in range(8):
                app[half, tile, c // 2, core, (c % 2) * 128 + s * 64:(c % 2) * 128 + s * 64 + 64] = (
                    applied[c * 64:(c + 1) * 64]
                )
        part = app.at[half, tile, :, core]
        copies = [remote(part, part, core_sem, tile, partner), remote(part, part, half_sem, tile, across)]
        for copy in copies:
            copy.start()
        return copies

    def forward_applied(tile):
        part = app.at[1 - half, tile, :, core]
        copy = remote(part, part, fwd_sem, tile, partner)
        copy.start()
        return copy

    at_home = pl.ds(pl.multiple_of(x * 512, 512), 512)
    from_left = pl.ds(pl.multiple_of(((x + 3) % 4) * 512, 512), 512)
    from_right = pl.ds(pl.multiple_of(((x + 1) % 4) * 512, 512), 512)

    def both_ways(first, second, sems, q):
        copies = [remote(first, first, sems, q * 2, right), remote(second, second, sems, q * 2 + 1, left)]
        for copy in copies:
            copy.start()
        return copies

    def rows_of(q):
        return (lg_top, 64) if q == 8 else (lg.at[q], 96)

    def ring(q):
        block = rows_of(q)[0].at[:, at_home]
        return both_ways(block, block, l2_sem, q)

    def forward(q):
        rows, count = rows_of(q)
        return both_ways(
            rows.at[pl.ds(0, count), from_left], rows.at[pl.ds(count, count), from_right], f_sem, q
        )

    sides = (half, 1 - half)

    def own_copies(q):
        o, b = OFFSETS[q // 2], q % 2
        return (
            remote(cq.at[o - 1, b, 0], rq.at[o - 1, b, 0], r1_sem, q, along_z[o]),
            remote(cs.at[o - 1, b, 0], rs.at[o - 1, b, 0], r1s_sem, q, along_z[o]),
        )

    def give_own(q):
        o, b = OFFSETS[q // 2], q % 2

        @pl.loop(0, 3)
        def _(tile):
            total = product(lg[q], app[half, tile].reshape(2048, 256))
            if o == 0:
                own[0, tile, b] = total
            else:
                values, scale = quantize(total, 0)
                cq[o - 1, b, 0, tile] = values
                cs[o - 1, b, 0, tile] = jnp.broadcast_to(scale, (8, 256))

        if o != 0:
            for copy in own_copies(q):
                copy.start()

    def other_copies(g, tile):
        o = OFFSETS[g]
        return (
            remote(cq.at[o - 1, :, 1, tile], rq.at[o - 1, :, 1, tile], r1b_sem, g * 3 + tile, along_z[o]),
            remote(cs.at[o - 1, :, 1, tile], rs.at[o - 1, :, 1, tile], r1bs_sem, g * 3 + tile, along_z[o]),
        )

    def give_other(g, tile):
        o = OFFSETS[g]
        total = product(
            lg[g * 2:g * 2 + 2].reshape(384, 2048), app[1 - half, tile].reshape(2048, 256)
        ).reshape(2, 192, 256)
        if o == 0:
            own[1, tile] = total
            return
        values, scale = quantize(total, 1)
        for b in range(2):
            cq[o - 1, b, 1, tile] = values[b]
            cs[o - 1, b, 1, tile] = jnp.broadcast_to(scale[b], (8, 256))
        for copy in other_copies(g, tile):
            copy.start()

    def make_top(turn, tile):
        total = product(lg_top[...], app[sides[turn], tile].reshape(2048, 256))
        ctop[turn, :, :, :, tile * 256:tile * 256 + 256] = total.reshape(4, 2, 16, 256)

    def top_copies(turn):
        return [
            remote(ctop.at[turn, (z + o) % 4], rtop.at[o - 1, turn], rt_sem, turn * 3 + o - 1, along_z[o])
            for o in (1, 2, 3)
        ]

    def give_top(turn):
        copies = top_copies(turn)
        for copy in copies:
            copy.start()
        return copies

    stage1, stage2, passed, applied, onward, tops = {}, {}, {}, {}, {}, {}

    def start_ring(q):
        stage1[q][0].wait()
        received(stage1[q][1])
        stage2[q] = ring(q)

    stage1[8] = exchange_top()
    stage1[0] = exchange(0)
    upper_copy.wait()
    applied[0] = apply(0)
    start_ring(8)
    start_ring(0)
    stage1[1] = exchange(1)
    applied[1] = apply(1)
    start_ring(1)
    stage1[2] = exchange(2)
    applied[2] = apply(2)
    received(stage2[8])
    passed[8] = forward(8)

    for q in range(8):
        received(stage2[q])
        passed[q] = forward(q)
        if q + 2 < 8:
            start_ring(q + 2)
        if q + 3 < 8:
            stage1[q + 3] = exchange(q + 3)
        if q == 0:
            received([applied[t][0] for t in range(3)])
            received(passed[8])
            for tile in range(3):
                make_top(0, tile)
            tops[0] = give_top(0)
        else:
            received(passed[q - 1])
            give_own(q - 1)
        if q == 3:
            applied[0][1].wait_recv()
            onward[0] = forward_applied(0)
        if q == 4:
            onward[0].wait_recv()
            make_top(1, 0)
            give_other(0, 0)
        if q == 5:
            applied[1][1].wait_recv()
            onward[1] = forward_applied(1)
            give_other(1, 0)
        if q == 6:
            onward[1].wait_recv()
            make_top(1, 1)
            give_other(0, 1)
            give_other(1, 1)
            give_other(2, 0)
        if q == 7:
            applied[2][1].wait_recv()
            onward[2] = forward_applied(2)
            give_other(2, 1)
    onward[2].wait_recv()
    make_top(1, 2)
    tops[1] = give_top(1)
    for g in range(3):
        give_other(g, 2)
    received(passed[7])
    give_own(7)

    received(tops[0])
    received(tops[1])
    for turn in range(2):
        total = ctop[turn, z]
        for o in range(3):
            total = total + rtop[o, turn]
        stop[turn] = total
    top_moves = [
        remote(stop.at[turn, row], ttop.at[t], r2t_sem, t, along_y[t])
        for t, (turn, row) in enumerate(((1, low), (0, 1 - low), (1, 1 - low)))
    ]
    for copy in top_moves:
        copy.start()
    for tile in range(3):
        give_other(3, tile)

    def chunk_sum(turn, row, tile):
        total = own[turn, tile, row]
        for o in range(3):
            total = total + rq[o, row, turn, tile].astype(jnp.float32) * rs[o, row, turn, tile, 0:1, :]
        return total

    moved = []

    def hand(t, turn, row, tile):
        values, scale = quantize(chunk_sum(turn, row, tile), 0)
        sq[t, tile] = values
        ss[t, tile] = jnp.broadcast_to(scale, (8, 256))
        copies = [
            remote(sq.at[t, tile], tq.at[t, tile], r2_sem, t * 3 + tile, along_y[t]),
            remote(ss.at[t, tile], ts.at[t, tile], r2s_sem, t * 3 + tile, along_y[t]),
        ]
        for copy in copies:
            copy.start()
        moved.extend(copies)

    for q in range(6):
        received(own_copies(q))
    for tile in range(3):
        hand(1, 0, 1 - low, tile)

    received(top_moves)
    @pl.when((depth != 0) | (core != 0))
    def _():
        for h in range(2):

            @pl.when((depth != 0) | (h == 0))
            def _():
                pltpu.make_async_remote_copy(
                    src_ref=ent_ref.at[pl.ds(0, 16)], dst_ref=ent_top.at[h],
                    send_sem=ent_sem.at[0, 0], recv_sem=ent_sem.at[1, h],
                    device_id=partner, device_id_type=MESH,
                ).wait_recv()

    top[core, half, z, low] = ent_top[half] - (stop[0, low] + ttop[1])
    top[core, 1 - half, z, low] = ent_top[1 - half] - (ttop[0] + ttop[2])
    gathers = []
    for o in range(1, 8):
        piece = top.at[core, :, z, low]
        copy = remote(piece, piece, tg_sem, o - 1, ((depth + o) % 8, core, col))
        copy.start()
        gathers.append(copy)

    for tile in range(3):
        for g in range(3):
            received(other_copies(g, tile))
        hand(0, 1, low, tile)
        hand(2, 1, 1 - low, tile)
        if tile == 0:
            received(gathers)
            core_copy = remote(top.at[core], top.at[core], tc_sem, 0, partner)
            core_copy.start()
    core_copy.wait_recv()

    @pl.when(col == 0)
    def _():
        row = lax.broadcasted_iota(jnp.int32, (PW, PW), 0)
        identity = (row == lax.broadcasted_iota(jnp.int32, (PW, PW), 1)).astype(jnp.float32)
        pivot = top[:, :, :, :, :, :PW].reshape(PW, PW)
        error = identity - pivot * (1.0 / 16.0)
        square = dot3(error, error)
        inverse[...] = dot3(identity + error, identity + square) * (1.0 / 16.0)

    def arrived(t, tile):
        return tq[t, tile].astype(jnp.float32) * ts[t, tile, 0:1, :]

    mine = pl.ds(pl.multiple_of(half * 192, 192), 192)
    other = pl.ds(pl.multiple_of((1 - half) * 192, 192), 192)
    received(moved[0:6])
    for tile in range(3):
        cols = slice(tile * 256, tile * 256 + 256)
        out_ref[mine, cols] = ent_ref[mine, cols] - (chunk_sum(0, low, tile) + arrived(1, tile))
    for tile in range(3):
        received(moved[6 + tile * 4:10 + tile * 4])
        cols = slice(tile * 256, tile * 256 + 256)
        out_ref[other, cols] = ent_ref[other, cols] - (arrived(0, tile) + arrived(2, tile))

    def cf_copy(o):
        piece = cf.at[o]
        return remote(piece, piece, cf_sem, o - 1, (depth, core, o))

    def zero_copy(o):
        piece = cf.at[0]
        return remote(piece, piece, cf_sem, 6 + o, (depth, core, o))

    @pl.when(col == 0)
    def _():
        cf[...] = dot3(out_ref[:, :PW], inverse[...]).reshape(8, 48, PW)
        for o in range(1, 8):
            cf_copy(o).start()
        for o in range(1, 8):
            zero_copy(o).start()

    for tile in range(3):
        cols = slice(tile * 256, tile * 256 + 256)
        high, rest = split(top[:, :, :, :, :, cols].reshape(PW, 256))
        top_high[:, cols] = high
        top_low[:, cols] = rest

    @pl.when(col == 0)
    def _():
        for o in range(1, 8):
            cf_copy(o).wait_send()
            zero_copy(o).wait_send()

    def ring_copy(o, target):
        piece = cf.at[col]
        return remote(piece, piece, cg_sem, o - 1, (depth, core, target))

    for c in range(1, 8):

        @pl.when(col == c)
        def _():
            cf_copy(c).wait_recv()
            copies = []
            for o in range(1, 7):
                copy = ring_copy(o, (c - 1 + o) % 7 + 1)
                copy.start()
                copies.append(copy)
            zero_copy(c).wait_recv()
            for copy in copies:
                copy.wait()

    column = cf[...].reshape(384, PW)
    cf_ref[...] = column
    column_high, column_low = split(column)
    for tile in range(3):
        cols = slice(tile * 256, tile * 256 + 256)
        th, tl = top_high[:, cols], top_low[:, cols]
        out_ref[:, cols] = out_ref[:, cols] - (
            product(column_high, th) + (product(column_high, tl) + product(column_low, th))
        )

    for group in (
        *(sends for _, sends in stage1.values()), *stage2.values(), *passed.values(), *applied.values(),
        onward.values(), tops[0], tops[1], top_moves, gathers, [core_copy], moved,
    ):
        for copy in group:
            copy.wait_send()
    for q in range(6):
        for copy in own_copies(q):
            copy.wait_send()
    for g in range(3):
        for tile in range(3):
            for copy in other_copies(g, tile):
                copy.wait_send()
    entries(lambda copy: copy.wait_send())


def sems(count):
    return pltpu.SemaphoreType.DMA((2, count))


def local(lower_panels, upper_panels, given_inverse, structure, ancestor_entries):
    f32, bf16, i16 = jnp.float32, jnp.bfloat16, jnp.int16
    return pl.pallas_call(
        whole_kernel,
        name="whole",
        out_shape=(jax.ShapeDtypeStruct((384, PW), f32), jax.ShapeDtypeStruct((384, 768), f32)),
        in_specs=[pl.BlockSpec(memory_space=pltpu.SMEM)] + [VMEM] * 4,
        out_specs=(VMEM, VMEM),
        scratch_shapes=[
            pltpu.VMEM((2, 512, 768), bf16),
            pltpu.VMEM((8, 2, 2, 192, 128), bf16),
            pltpu.VMEM((2, 2, 128, 128), bf16),
            pltpu.VMEM((2, 3, 4, 2, 256, 256), bf16),
            pltpu.VMEM((8, 192, 2048), bf16),
            pltpu.VMEM((128, 2048), bf16),
            pltpu.VMEM((3, 2, 2, 3, 192, 256), i16),
            pltpu.VMEM((3, 2, 2, 3, 8, 256), f32),
            pltpu.VMEM((3, 2, 2, 3, 192, 256), i16),
            pltpu.VMEM((3, 2, 2, 3, 8, 256), f32),
            pltpu.VMEM((2, 3, 2, 192, 256), f32),
            pltpu.VMEM((3, 3, 192, 256), i16),
            pltpu.VMEM((3, 3, 8, 256), f32),
            pltpu.VMEM((3, 3, 192, 256), i16),
            pltpu.VMEM((3, 3, 8, 256), f32),
            pltpu.VMEM((2, 16, 768), f32),
            pltpu.VMEM((2, 4, 2, 16, 768), f32),
            pltpu.VMEM((3, 2, 2, 16, 768), f32),
            pltpu.VMEM((2, 2, 16, 768), f32),
            pltpu.VMEM((3, 16, 768), f32),
            pltpu.VMEM((2, 2, 4, 2, 16, 768), f32),
            pltpu.VMEM((PW, 768), bf16),
            pltpu.VMEM((PW, 768), bf16),
            pltpu.VMEM((PW, PW), f32),
            pltpu.VMEM((8, 48, PW), f32),
            sems(1), sems(27), pltpu.SemaphoreType.DMA((9,)), sems(18), sems(18), sems(3), sems(3), sems(3),
            sems(6), sems(6), sems(9), sems(9), sems(9), sems(9),
            sems(32), sems(6), sems(3), sems(7), sems(1), sems(14), sems(6),
        ],
        compiler_params=pltpu.CompilerParams(collective_id=0, has_side_effects=True, vmem_limit_bytes=LIMIT),
    )(structure, jnp.swapaxes(lower_panels, 2, 3), upper_panels, given_inverse, ancestor_entries)


def solution(mesh):
    return jax.shard_map(
        local,
        mesh=mesh,
        in_specs=(
            P("depth", None, None, ("rows", "cols")),
            P("depth", "rows", "cols"),
            P("depth", "rows", None),
            P("depth", None),
            P(("depth", "rows"), "cols"),
        ),
        out_specs=(P(("depth", "rows"), None), P(("depth", "rows"), "cols")),
        check_vma=False,
    )
```

time: 563 us -> 184 us (0.33)
  waiting for transfers between devices: 492 us -> 0 us
  Pallas kernels: 0 us -> 176 us
  matrix products: 33.9 us -> 0 us
  other arithmetic: 14 us -> 0 us
  between operations: 13.9 us -> 0.65 us
    psum x2 -> x0, waiting for transfers between devices: 223 us -> none  [the longest x1 122 us: local(): top_block = lax.psum(picked, ('depth', 'rows'))]
    pallas_call x0 -> x1, Pallas kernels: none -> 176 us  [local(): pl.pallas_call(whole_kernel, name='whole', out_shape=(jax.ShapeDtypeStruc...]
    all_gather x2 -> x0, waiting for transfers between devices: 161 us -> none  [the longest x1 147 us: local(): lax.all_gather(lower_masked, 'cols', axis=3, tiled=True)]
    reduce_scatter x1 -> x0, waiting for transfers between devices: 108 us -> none  [local(): lax.psum_scatter(negated, ('depth', 'rows'), scatter_dimension=0, tiled=T...]
    dot_general x7 -> x0, matrix products: 33.9 us -> none  [the longest x1 20.8 us: local(): jnp.einsum('sjqk,skc->jqc', lax.all_gather(lower_masked, 'cols', axis=3,...]
    select_n x4 -> x0, other arithmetic: 6.07 us -> none  [the longest x2 3.28 us: from_root(): return lax.psum(jnp.where(mine, array, jnp.zeros_like(array)), axis)]
  transfers between devices with their start and end apart: 5 -> 0, of which waited for: 5 -> 0; matrix products, arithmetic and copies ran while one was open for 1% -> 0% of each run, Pallas kernels for 0% -> 0%
where the time goes in v2:
time: 184 us; the launch traced here: 180 us
  Pallas kernels  176 us (96%)
  local copies, waits for them, and re-layouts  3.18 us (2%)
    pallas_call x1, Pallas kernels, local(): pl.pallas_call(whole_kernel, name='whole', out_shape=(jax.ShapeDtypeStruc...  176 us

profile of v2, /device:TPU:111, one launch (start us, length us, event | category | flops | bytes accessed | tf_op | source)
XLA Modules:
  0.0 180.2 jit_solution(17909843410962232994)
XLA Ops:
  0.6 176.4 %whole.1 = (f32[384,512]{1,0:T(8,128)}, f32[384,768]{1,0:T(8,128)}) custom-call(s32[2,48]{1,0:T(2,128)} %kept_ref.1, bf16[2,8,64,768]{3,2,1,0:T(8,128)(2,1)} %bitcast.1, bf16[2,512,768]{2,1,0:T(8,128)(2,1)} %up_ref.1, bf16[2,512,1024]{2,1,0:T(8,128)(2,1)} %inv_ref.1, f32[384,768]{1,0:T(8,128)} %ent_ref.1), custom_call_target="tpu_custom_call" | custom-call | tf_op jit(solution)/shard_map/whole/pallas_call | solution.py:514
  177.1 0.0 copy-start
  177.1 2.2 %copy.9 = f32[384,512]{1,0:T(8,128)} copy(f32[384,512]{1,0:T(8,128)} %get-tuple-element.4) | data formatting | bytes 1572864
  179.2 0.0 copy-done
  179.2 1.0 copy.10
Async XLA Ops:
  177.1 2.2 %copy-start = (f32[384,768]{1,0:T(8,128)S(1)}, f32[384,768]{1,0:T(8,128)}, u32[]{:S(2)}) copy-start(f32[384,768]{1,0:T(8,128)} %get-tuple-element.5) | copy-start | bytes 3538948

commit v3 on v2

--- a/solution.py
+++ b/solution.py
@@ -83,10 +83,7 @@
     friends += [across_core, along_y[2]]
     for friend in friends:
         pl.semaphore_signal(barrier, inc=1, device_id=friend, device_id_type=MESH)
-    pl.semaphore_wait(barrier, len(friends))
-
     upper_copy = remote(up_ref, up_other, up_sem, 0, partner)
-    upper_copy.start()
 
     def entry_copy(g, row):
         target = ((g % 2) * 4 + (g // 2) % 4, g // 16, col)
@@ -108,14 +105,18 @@
                 for g in groups[c]:
                     act(entry_copy(g, g - 24 * c))
 
-    entries(lambda copy: copy.start())
-    for c in range(2):
-
-        @pl.when(holder[c])
+    def wait_entries():
+        @pl.when((depth != 0) | (core != 0))
         def _():
-            for g, h in stays[c]:
-                row = (g - 24 * c) * 16
-                ent_top[h] = ent_ref[row:row + 16, :]
+            for h in range(2):
+
+                @pl.when((depth != 0) | (h == 0))
+                def _():
+                    pltpu.make_async_remote_copy(
+                        src_ref=ent_ref.at[pl.ds(0, 16)], dst_ref=ent_top.at[h],
+                        send_sem=ent_sem.at[0, 0], recv_sem=ent_sem.at[1, h],
+                        device_id=partner, device_id_type=MESH,
+                    ).wait_recv()
 
     def factor(s, block):
         return jnp.full((1, 128), kept_ref[s, block].astype(jnp.float32), jnp.float32)
@@ -140,12 +141,14 @@
             sends.append(copy)
         return here, sends
 
-    def exchange_top():
+    def turn_top():
         for part in range(4):
             turned_top[part // 2, part % 2] = turn_over(0, part)
+
+    def share_top():
         return share(lambda r, h: turned_top.at[r, h], lg_top.at[:, pl.ds(lane, 128)], 24)
 
-    def exchange(q):
+    def turn_rows(q):
         j = (q % 2) * 4 + (z + OFFSETS[q // 2]) % 4
         for part in range(6):
             value = turn_over(j, part)
@@ -154,6 +157,8 @@
                 turned[q, row // 384, (row // 192) % 2, row % 192:row % 192 + 64] = (
                     value[piece * 64:piece * 64 + 64]
                 )
+
+    def share_rows(q):
         return share(lambda r, h: turned.at[q, r, h], lg.at[q, :, pl.ds(lane, 128)], q * 3)
 
     mine, theirs = pl.multiple_of(core * 512, 512), pl.multiple_of((1 - core) * 512, 512)
@@ -173,8 +178,7 @@
                 )
         part = app.at[half, tile, :, core]
         copies = [remote(part, part, core_sem, tile, partner), remote(part, part, half_sem, tile, across)]
-        for copy in copies:
-            copy.start()
+        copies[0].start()
         return copies
 
     def forward_applied(tile):
@@ -277,28 +281,45 @@
         received(stage1[q][1])
         stage2[q] = ring(q)
 
-    stage1[8] = exchange_top()
-    stage1[0] = exchange(0)
+    turn_top()
+    turn_rows(0)
+    pl.semaphore_wait(barrier, len(friends))
+    stage1[8] = share_top()
+    stage1[0] = share_rows(0)
+    upper_copy.start()
+    for q in range(1, 4):
+        turn_rows(q)
+        stage1[q] = share_rows(q)
+    start_ring(8)
+    start_ring(0)
+    entries(lambda copy: copy.start())
+    for c in range(2):
+
+        @pl.when(holder[c])
+        def _():
+            for g, h in stays[c]:
+                row = (g - 24 * c) * 16
+                ent_top[h] = ent_ref[row:row + 16, :]
+
     upper_copy.wait()
     applied[0] = apply(0)
-    start_ring(8)
-    start_ring(0)
-    stage1[1] = exchange(1)
-    applied[1] = apply(1)
     start_ring(1)
-    stage1[2] = exchange(2)
-    applied[2] = apply(2)
+    for q in range(4, 8):
+        turn_rows(q)
+        stage1[q] = share_rows(q)
+    applied[0][1].start()
     received(stage2[8])
     passed[8] = forward(8)
+    applied[1] = apply(1)
+    applied[2] = apply(2)
 
     for q in range(8):
         received(stage2[q])
         passed[q] = forward(q)
         if q + 2 < 8:
             start_ring(q + 2)
-        if q + 3 < 8:
-            stage1[q + 3] = exchange(q + 3)
         if q == 0:
+            applied[1][1].start()
             received([applied[t][0] for t in range(3)])
             received(passed[8])
             for tile in range(3):
@@ -307,32 +328,29 @@
         else:
             received(passed[q - 1])
             give_own(q - 1)
+        if q in (2, 4, 6):
+            tile = q // 2 - 1
+            applied[tile][1].wait_recv()
+            onward[tile] = forward_applied(tile)
+        if q == 2:
+            applied[2][1].start()
+        if q in (3, 5, 7):
+            onward[q // 2 - 1].wait_recv()
+            make_top(1, q // 2 - 1)
         if q == 3:
-            applied[0][1].wait_recv()
-            onward[0] = forward_applied(0)
+            give_other(0, 0)
         if q == 4:
-            onward[0].wait_recv()
-            make_top(1, 0)
-            give_other(0, 0)
+            give_other(1, 0)
         if q == 5:
-            applied[1][1].wait_recv()
-            onward[1] = forward_applied(1)
-            give_other(1, 0)
-        if q == 6:
-            onward[1].wait_recv()
-            make_top(1, 1)
             give_other(0, 1)
             give_other(1, 1)
+        if q == 6:
             give_other(2, 0)
+            give_other(2, 1)
         if q == 7:
-            applied[2][1].wait_recv()
-            onward[2] = forward_applied(2)
-            give_other(2, 1)
-    onward[2].wait_recv()
-    make_top(1, 2)
-    tops[1] = give_top(1)
-    for g in range(3):
-        give_other(g, 2)
+            tops[1] = give_top(1)
+            for g in range(3):
+                give_other(g, 2)
     received(passed[7])
     give_own(7)
 
@@ -378,17 +396,7 @@
         hand(1, 0, 1 - low, tile)
 
     received(top_moves)
-    @pl.when((depth != 0) | (core != 0))
-    def _():
-        for h in range(2):
-
-            @pl.when((depth != 0) | (h == 0))
-            def _():
-                pltpu.make_async_remote_copy(
-                    src_ref=ent_ref.at[pl.ds(0, 16)], dst_ref=ent_top.at[h],
-                    send_sem=ent_sem.at[0, 0], recv_sem=ent_sem.at[1, h],
-                    device_id=partner, device_id_type=MESH,
-                ).wait_recv()
+    wait_entries()
 
     top[core, half, z, low] = ent_top[half] - (stop[0, low] + ttop[1])
     top[core, 1 - half, z, low] = ent_top[1 - half] - (ttop[0] + ttop[2])
@@ -433,21 +441,23 @@
         cols = slice(tile * 256, tile * 256 + 256)
         out_ref[other, cols] = ent_ref[other, cols] - (arrived(0, tile) + arrived(2, tile))
 
-    def cf_copy(o):
-        piece = cf.at[o]
-        return remote(piece, piece, cf_sem, o - 1, (depth, core, o))
-
-    def zero_copy(o):
-        piece = cf.at[0]
-        return remote(piece, piece, cf_sem, 6 + o, (depth, core, o))
+    def piece(c):
+        return cf.at[(c - 1) * 56:min(c * 56, 384)]
+
+    def cf_copy(c):
+        return remote(piece(c), piece(c), cf_sem, c - 1, (depth, core, c))
+
+    def hand_on(c, target):
+        return pltpu.make_async_remote_copy(
+            src_ref=piece(c), dst_ref=piece(c), send_sem=cg_sem.at[0, target - 1], recv_sem=cg_sem.at[1, c - 1],
+            device_id=(depth, core, target), device_id_type=MESH,
+        )
 
     @pl.when(col == 0)
     def _():
-        cf[...] = dot3(out_ref[:, :PW], inverse[...]).reshape(8, 48, PW)
-        for o in range(1, 8):
-            cf_copy(o).start()
-        for o in range(1, 8):
-            zero_copy(o).start()
+        cf[...] = dot3(out_ref[:, :PW], inverse[...])
+        for c in (4, 5, 2, 3, 6, 7, 1):
+            cf_copy(c).start()
 
     for tile in range(3):
         cols = slice(tile * 256, tile * 256 + 256)
@@ -457,29 +467,24 @@
 
     @pl.when(col == 0)
     def _():
-        for o in range(1, 8):
-            cf_copy(o).wait_send()
-            zero_copy(o).wait_send()
-
-    def ring_copy(o, target):
-        piece = cf.at[col]
-        return remote(piece, piece, cg_sem, o - 1, (depth, core, target))
+        for c in range(1, 8):
+            cf_copy(c).wait_send()
 
     for c in range(1, 8):
 
         @pl.when(col == c)
         def _():
             cf_copy(c).wait_recv()
-            copies = []
-            for o in range(1, 7):
-                copy = ring_copy(o, (c - 1 + o) % 7 + 1)
+            others = [k for k in range(1, 8) if k != c]
+            copies = [hand_on(c, k) for k in others]
+            for copy in copies:
                 copy.start()
-                copies.append(copy)
-            zero_copy(c).wait_recv()
+            for k in others:
+                hand_on(k, k).wait_recv()
             for copy in copies:
-                copy.wait()
-
-    column = cf[...].reshape(384, PW)
+                copy.wait_send()
+
+    column = cf[...]
     cf_ref[...] = column
     column_high, column_low = split(column)
     for tile in range(3):
@@ -542,10 +547,10 @@
             pltpu.VMEM((PW, 768), bf16),
             pltpu.VMEM((PW, 768), bf16),
             pltpu.VMEM((PW, PW), f32),
-            pltpu.VMEM((8, 48, PW), f32),
+            pltpu.VMEM((384, PW), f32),
             sems(1), sems(27), pltpu.SemaphoreType.DMA((9,)), sems(18), sems(18), sems(3), sems(3), sems(3),
             sems(6), sems(6), sems(9), sems(9), sems(9), sems(9),
-            sems(32), sems(6), sems(3), sems(7), sems(1), sems(14), sems(6),
+            sems(32), sems(6), sems(3), sems(7), sems(1), sems(7), sems(14),
         ],
         compiler_params=pltpu.CompilerParams(collective_id=0, has_side_effects=True, vmem_limit_bytes=LIMIT),
     )(structure, jnp.swapaxes(lower_panels, 2, 3), upper_panels, given_inverse, ancestor_entries)

time: 184 us -> 161 us (0.88); the launches traced: 180 us -> 160 us
  Pallas kernels: 176 us -> 156 us
    pallas_call x1, Pallas kernels: 176 us -> 156 us  [local(): pl.pallas_call(whole_kernel, name='whole', out_shape=(jax.ShapeDtypeStruc...]
where the time goes in v3:
time: 161 us; the launch traced here: 160 us
  Pallas kernels  156 us (97%)
  local copies, waits for them, and re-layouts  3.18 us (2%)
    pallas_call x1, Pallas kernels, local(): pl.pallas_call(whole_kernel, name='whole', out_shape=(jax.ShapeDtypeStruc...  156 us

profile of v3, /device:TPU:111, one launch (start us, length us, event | category | flops | bytes accessed | tf_op | source)
XLA Modules:
  0.0 160.2 jit_solution(6478923465566876261)
XLA Ops:
  0.6 156.4 %whole.1 = (f32[384,512]{1,0:T(8,128)}, f32[384,768]{1,0:T(8,128)}) custom-call(s32[2,48]{1,0:T(2,128)} %kept_ref.1, bf16[2,8,64,768]{3,2,1,0:T(8,128)(2,1)} %bitcast.1, bf16[2,512,768]{2,1,0:T(8,128)(2,1)} %up_ref.1, bf16[2,512,1024]{2,1,0:T(8,128)(2,1)} %inv_ref.1, f32[384,768]{1,0:T(8,128)} %ent_ref.1), custom_call_target="tpu_custom_call" | custom-call | tf_op jit(solution)/shard_map/whole/pallas_call | solution.py:519
  157.0 0.0 copy-start
  157.0 2.2 %copy.9 = f32[384,512]{1,0:T(8,128)} copy(f32[384,512]{1,0:T(8,128)} %get-tuple-element.4) | data formatting | bytes 1572864
  159.2 0.0 copy-done
  159.2 1.0 copy.10
Async XLA Ops:
  157.0 2.2 %copy-start = (f32[384,768]{1,0:T(8,128)S(1)}, f32[384,768]{1,0:T(8,128)}, u32[]{:S(2)}) copy-start(f32[384,768]{1,0:T(8,128)} %get-tuple-element.5) | copy-start | bytes 3538948

commit v4 on v3

--- a/solution.py
+++ b/solution.py
@@ -51,10 +51,10 @@
 def whole_kernel(
     kept_ref, low_ref, up_ref, inv_ref, ent_ref, cf_ref, out_ref,
     up_other, turned, turned_top, app, lg, lg_top, cq, cs, rq, rs, own, sq, ss, tq, ts,
-    ent_top, ctop, rtop, stop, ttop, top, top_high, top_low, inverse, cf,
+    ent_top, ctop, rtop, stop, ttop, top, top_high, top_low, inverse, cf, cf_scale,
     up_sem, l1_sem, loc_sem, l2_sem, f_sem, core_sem, half_sem, fwd_sem,
     r1_sem, r1s_sem, r1b_sem, r1bs_sem, r2_sem, r2s_sem,
-    ent_sem, rt_sem, r2t_sem, tg_sem, tc_sem, cf_sem, cg_sem,
+    ent_sem, rt_sem, r2t_sem, tg_sem, tc_sem, cf_sem, cfs_sem, cg_sem,
 ):
     low, z, core, x, half = place()
     depth, col = low * 4 + z, x * 2 + half
@@ -412,10 +412,24 @@
             received(other_copies(g, tile))
         hand(0, 1, low, tile)
         hand(2, 1, 1 - low, tile)
-        if tile == 0:
-            received(gathers)
-            core_copy = remote(top.at[core], top.at[core], tc_sem, 0, partner)
-            core_copy.start()
+    received(gathers)
+    core_copy = remote(top.at[core], top.at[core], tc_sem, 0, partner)
+    core_copy.start()
+
+    def arrived(t, tile):
+        return tq[t, tile].astype(jnp.float32) * ts[t, tile, 0:1, :]
+
+    mine = pl.ds(pl.multiple_of(half * 192, 192), 192)
+    other = pl.ds(pl.multiple_of((1 - half) * 192, 192), 192)
+    received(moved[0:6])
+    for tile in range(3):
+        cols = slice(tile * 256, tile * 256 + 256)
+        out_ref[mine, cols] = ent_ref[mine, cols] - (chunk_sum(0, low, tile) + arrived(1, tile))
+    for tile in range(3):
+        received(moved[6 + tile * 4:10 + tile * 4])
+        cols = slice(tile * 256, tile * 256 + 256)
+        out_ref[other, cols] = ent_ref[other, cols] - (arrived(0, tile) + arrived(2, tile))
+
     core_copy.wait_recv()
 
     @pl.when(col == 0)
@@ -427,22 +441,18 @@
         square = dot3(error, error)
         inverse[...] = dot3(identity + error, identity + square) * (1.0 / 16.0)
 
-    def arrived(t, tile):
-        return tq[t, tile].astype(jnp.float32) * ts[t, tile, 0:1, :]
-
-    mine = pl.ds(pl.multiple_of(half * 192, 192), 192)
-    other = pl.ds(pl.multiple_of((1 - half) * 192, 192), 192)
-    received(moved[0:6])
-    for tile in range(3):
-        cols = slice(tile * 256, tile * 256 + 256)
-        out_ref[mine, cols] = ent_ref[mine, cols] - (chunk_sum(0, low, tile) + arrived(1, tile))
-    for tile in range(3):
-        received(moved[6 + tile * 4:10 + tile * 4])
-        cols = slice(tile * 256, tile * 256 + 256)
-        out_ref[other, cols] = ent_ref[other, cols] - (arrived(0, tile) + arrived(2, tile))
+    bounds = (0, 64, 128, 192, 240, 288, 336, 384)
 
     def piece(c):
-        return cf.at[(c - 1) * 56:min(c * 56, 384)]
+        return cf.at[bounds[c - 1]:bounds[c]]
+
+    def scale_copy(c):
+        return remote(cf_scale, cf_scale, cfs_sem, c - 1, (depth, core, c))
+
+    first_row = depth * 768 + core * 384
+    unit = (
+        lax.broadcasted_iota(jnp.int32, (384, PW), 0) + first_row == lax.broadcasted_iota(jnp.int32, (384, PW), 1)
+    ).astype(jnp.float32)
 
     def cf_copy(c):
         return remote(piece(c), piece(c), cf_sem, c - 1, (depth, core, c))
@@ -455,9 +465,13 @@
 
     @pl.when(col == 0)
     def _():
-        cf[...] = dot3(out_ref[:, :PW], inverse[...])
+        values, scale = quantize(dot3(out_ref[:, :PW], inverse[...]) - unit, 0)
+        cf[...] = values
+        cf_scale[...] = jnp.broadcast_to(scale, (8, PW))
         for c in (4, 5, 2, 3, 6, 7, 1):
             cf_copy(c).start()
+        for c in range(1, 8):
+            scale_copy(c).start()
 
     for tile in range(3):
         cols = slice(tile * 256, tile * 256 + 256)
@@ -469,6 +483,7 @@
     def _():
         for c in range(1, 8):
             cf_copy(c).wait_send()
+            scale_copy(c).wait_send()
 
     for c in range(1, 8):
 
@@ -481,10 +496,11 @@
                 copy.start()
             for k in others:
                 hand_on(k, k).wait_recv()
+            scale_copy(c).wait_recv()
             for copy in copies:
                 copy.wait_send()
 
-    column = cf[...]
+    column = cf[...].astype(jnp.float32) * cf_scale[0:1, :] + unit
     cf_ref[...] = column
     column_high, column_low = split(column)
     for tile in range(3):
@@ -547,10 +563,11 @@
             pltpu.VMEM((PW, 768), bf16),
             pltpu.VMEM((PW, 768), bf16),
             pltpu.VMEM((PW, PW), f32),
-            pltpu.VMEM((384, PW), f32),
+            pltpu.VMEM((384, PW), i16),
+            pltpu.VMEM((8, PW), f32),
             sems(1), sems(27), pltpu.SemaphoreType.DMA((9,)), sems(18), sems(18), sems(3), sems(3), sems(3),
             sems(6), sems(6), sems(9), sems(9), sems(9), sems(9),
-            sems(32), sems(6), sems(3), sems(7), sems(1), sems(7), sems(14),
+            sems(32), sems(6), sems(3), sems(7), sems(1), sems(7), sems(7), sems(7),
         ],
         compiler_params=pltpu.CompilerParams(collective_id=0, has_side_effects=True, vmem_limit_bytes=LIMIT),
     )(structure, jnp.swapaxes(lower_panels, 2, 3), upper_panels, given_inverse, ancestor_entries)

time: 161 us -> 151 us (0.938)
  Pallas kernels: 156 us -> 147 us
    pallas_call x1, Pallas kernels: 156 us -> 147 us  [local(): pl.pallas_call(whole_kernel, name='whole', out_shape=(jax.ShapeDtypeStruc...]
where the time goes in v4:
time: 151 us
  Pallas kernels  147 us (97%)
  local copies, waits for them, and re-layouts  3.18 us (2%)
    pallas_call x1, Pallas kernels, local(): pl.pallas_call(whole_kernel, name='whole', out_shape=(jax.ShapeDtypeStruc...  147 us
    unnamed x4, local copies, waits for them, and re-layouts  3.18 us

profile of v4, /device:TPU:111, one launch (start us, length us, event | category | flops | bytes accessed | tf_op | source)
XLA Modules:
  0.0 150.9 jit_solution(12620196460775485746)
XLA Ops:
  0.6 147.0 %whole.1 = (f32[384,512]{1,0:T(8,128)}, f32[384,768]{1,0:T(8,128)}) custom-call(s32[2,48]{1,0:T(2,128)} %kept_ref.1, bf16[2,8,64,768]{3,2,1,0:T(8,128)(2,1)} %bitcast.1, bf16[2,512,768]{2,1,0:T(8,128)(2,1)} %up_ref.1, bf16[2,512,1024]{2,1,0:T(8,128)(2,1)} %inv_ref.1, f32[384,768]{1,0:T(8,128)} %ent_ref.1), custom_call_target="tpu_custom_call" | custom-call | tf_op jit(solution)/shard_map/whole/pallas_call | solution.py:535
  147.7 0.0 copy-start
  147.7 2.2 %copy.9 = f32[384,512]{1,0:T(8,128)} copy(f32[384,512]{1,0:T(8,128)} %get-tuple-element.4) | data formatting | bytes 1572864
  149.8 0.0 copy-done
  149.8 1.0 copy.10
Async XLA Ops:
  147.7 2.2 %copy-start = (f32[384,768]{1,0:T(8,128)S(1)}, f32[384,768]{1,0:T(8,128)}, u32[]{:S(2)}) copy-start(f32[384,768]{1,0:T(8,128)} %get-tuple-element.5) | copy-start | bytes 3538948

commit v5 on v4

--- a/solution.py
+++ b/solution.py
@@ -274,6 +274,36 @@
             copy.start()
         return copies
 
+    def sum_top():
+        received(tops[0])
+        received(tops[1])
+        for turn in range(2):
+            total = ctop[turn, z]
+            for o in range(3):
+                total = total + rtop[o, turn]
+            stop[turn] = total
+        top_moves = [
+            remote(stop.at[turn, row], ttop.at[t], r2t_sem, t, along_y[t])
+            for t, (turn, row) in enumerate(((1, low), (0, 1 - low), (1, 1 - low)))
+        ]
+        for copy in top_moves:
+            copy.start()
+        return top_moves
+
+    def gather_top():
+        received(top_moves)
+        wait_entries()
+
+        top[core, half, z, low] = ent_top[half] - (stop[0, low] + ttop[1])
+        top[core, 1 - half, z, low] = ent_top[1 - half] - (ttop[0] + ttop[2])
+        gathers = []
+        for o in range(1, 8):
+            piece = top.at[core, :, z, low]
+            copy = remote(piece, piece, tg_sem, o - 1, ((depth + o) % 8, core, col))
+            copy.start()
+            gathers.append(copy)
+        return gathers
+
     stage1, stage2, passed, applied, onward, tops = {}, {}, {}, {}, {}, {}
 
     def start_ring(q):
@@ -304,14 +334,19 @@
     upper_copy.wait()
     applied[0] = apply(0)
     start_ring(1)
-    for q in range(4, 8):
+    for q in range(4, 6):
         turn_rows(q)
         stage1[q] = share_rows(q)
     applied[0][1].start()
+    for q in range(6, 8):
+        turn_rows(q)
+        stage1[q] = share_rows(q)
     received(stage2[8])
     passed[8] = forward(8)
     applied[1] = apply(1)
+    applied[1][1].start()
     applied[2] = apply(2)
+    applied[2][1].start()
 
     for q in range(8):
         received(stage2[q])
@@ -319,7 +354,6 @@
         if q + 2 < 8:
             start_ring(q + 2)
         if q == 0:
-            applied[1][1].start()
             received([applied[t][0] for t in range(3)])
             received(passed[8])
             for tile in range(3):
@@ -328,45 +362,32 @@
         else:
             received(passed[q - 1])
             give_own(q - 1)
-        if q in (2, 4, 6):
-            tile = q // 2 - 1
+        if q in (1, 3, 5):
+            tile = q // 2
             applied[tile][1].wait_recv()
             onward[tile] = forward_applied(tile)
-        if q == 2:
-            applied[2][1].start()
-        if q in (3, 5, 7):
+        if q in (2, 4, 6):
             onward[q // 2 - 1].wait_recv()
             make_top(1, q // 2 - 1)
-        if q == 3:
+        if q == 2:
             give_other(0, 0)
         if q == 4:
             give_other(1, 0)
+            give_other(0, 1)
         if q == 5:
-            give_other(0, 1)
             give_other(1, 1)
         if q == 6:
+            tops[1] = give_top(1)
             give_other(2, 0)
+        if q == 7:
+            top_moves = sum_top()
+            give_other(0, 2)
+            give_other(1, 2)
+            gathers = gather_top()
             give_other(2, 1)
-        if q == 7:
-            tops[1] = give_top(1)
-            for g in range(3):
-                give_other(g, 2)
+            give_other(2, 2)
     received(passed[7])
     give_own(7)
-
-    received(tops[0])
-    received(tops[1])
-    for turn in range(2):
-        total = ctop[turn, z]
-        for o in range(3):
-            total = total + rtop[o, turn]
-        stop[turn] = total
-    top_moves = [
-        remote(stop.at[turn, row], ttop.at[t], r2t_sem, t, along_y[t])
-        for t, (turn, row) in enumerate(((1, low), (0, 1 - low), (1, 1 - low)))
-    ]
-    for copy in top_moves:
-        copy.start()
     for tile in range(3):
         give_other(3, tile)
 
@@ -394,18 +415,6 @@
         received(own_copies(q))
     for tile in range(3):
         hand(1, 0, 1 - low, tile)
-
-    received(top_moves)
-    wait_entries()
-
-    top[core, half, z, low] = ent_top[half] - (stop[0, low] + ttop[1])
-    top[core, 1 - half, z, low] = ent_top[1 - half] - (ttop[0] + ttop[2])
-    gathers = []
-    for o in range(1, 8):
-        piece = top.at[core, :, z, low]
-        copy = remote(piece, piece, tg_sem, o - 1, ((depth + o) % 8, core, col))
-        copy.start()
-        gathers.append(copy)
 
     for tile in range(3):
         for g in range(3):

time: 151 us -> 145 us (0.960); the launches traced: 151 us -> 142 us
  Pallas kernels: 147 us -> 139 us
    pallas_call x1, Pallas kernels: 147 us -> 139 us  [local(): pl.pallas_call(whole_kernel, name='whole', out_shape=(jax.ShapeDtypeStruc...]
where the time goes in v5:
time: 145 us; the launch traced here: 142 us
  Pallas kernels  139 us (96%)
  local copies, waits for them, and re-layouts  3.18 us (2%)
    pallas_call x1, Pallas kernels, local(): pl.pallas_call(whole_kernel, name='whole', out_shape=(jax.ShapeDtypeStruc...  139 us
    unnamed x4, local copies, waits for them, and re-layouts  3.18 us

profile of v5, /device:TPU:111, one launch (start us, length us, event | category | flops | bytes accessed | tf_op | source)
XLA Modules:
  0.0 142.5 jit_solution(15368420548316111570)
XLA Ops:
  0.6 138.6 %whole.1 = (f32[384,512]{1,0:T(8,128)}, f32[384,768]{1,0:T(8,128)}) custom-call(s32[2,48]{1,0:T(2,128)} %kept_ref.1, bf16[2,8,64,768]{3,2,1,0:T(8,128)(2,1)} %bitcast.1, bf16[2,512,768]{2,1,0:T(8,128)(2,1)} %up_ref.1, bf16[2,512,1024]{2,1,0:T(8,128)(2,1)} %inv_ref.1, f32[384,768]{1,0:T(8,128)} %ent_ref.1), custom_call_target="tpu_custom_call" | custom-call | tf_op jit(solution)/shard_map/whole/pallas_call | solution.py:544
  139.3 0.0 copy-start
  139.3 2.2 %copy.9 = f32[384,512]{1,0:T(8,128)} copy(f32[384,512]{1,0:T(8,128)} %get-tuple-element.4) | data formatting | bytes 1572864
  141.4 0.0 copy-done
  141.4 1.0 copy.10
Async XLA Ops:
  139.3 2.2 %copy-start = (f32[384,768]{1,0:T(8,128)S(1)}, f32[384,768]{1,0:T(8,128)}, u32[]{:S(2)}) copy-start(f32[384,768]{1,0:T(8,128)} %get-tuple-element.5) | copy-start | bytes 3538948

commit v6 on v5

--- a/solution.py
+++ b/solution.py
@@ -421,9 +421,10 @@
             received(other_copies(g, tile))
         hand(0, 1, low, tile)
         hand(2, 1, 1 - low, tile)
-    received(gathers)
-    core_copy = remote(top.at[core], top.at[core], tc_sem, 0, partner)
-    core_copy.start()
+        if tile == 1:
+            received(gathers)
+            core_copy = remote(top.at[core], top.at[core], tc_sem, 0, partner)
+            core_copy.start()
 
     def arrived(t, tile):
         return tq[t, tile].astype(jnp.float32) * ts[t, tile, 0:1, :]

time: 145 us -> 145 us (level)
  no operation moved by 1% of the time
where the time goes in v6:
time: 145 us; the launch traced here: 142 us
  Pallas kernels  139 us (96%)
  local copies, waits for them, and re-layouts  3.18 us (2%)
    pallas_call x1, Pallas kernels, local(): pl.pallas_call(whole_kernel, name='whole', out_shape=(jax.ShapeDtypeStruc...  139 us
    unnamed x4, local copies, waits for them, and re-layouts  3.18 us

profile of v6, /device:TPU:111, one launch (start us, length us, event | category | flops | bytes accessed | tf_op | source)
XLA Modules:
  0.0 142.5 jit_solution(7776736480841725549)
XLA Ops:
  0.6 138.6 %whole.1 = (f32[384,512]{1,0:T(8,128)}, f32[384,768]{1,0:T(8,128)}) custom-call(s32[2,48]{1,0:T(2,128)} %kept_ref.1, bf16[2,8,64,768]{3,2,1,0:T(8,128)(2,1)} %bitcast.1, bf16[2,512,768]{2,1,0:T(8,128)(2,1)} %up_ref.1, bf16[2,512,1024]{2,1,0:T(8,128)(2,1)} %inv_ref.1, f32[384,768]{1,0:T(8,128)} %ent_ref.1), custom_call_target="tpu_custom_call" | custom-call | tf_op jit(solution)/shard_map/whole/pallas_call | solution.py:545
  139.3 0.0 copy-start
  139.3 2.2 %copy.9 = f32[384,512]{1,0:T(8,128)} copy(f32[384,512]{1,0:T(8,128)} %get-tuple-element.4) | data formatting | bytes 1572864
  141.4 0.0 copy-done
  141.4 1.0 copy.10
Async XLA Ops:
  139.3 2.2 %copy-start = (f32[384,768]{1,0:T(8,128)S(1)}, f32[384,768]{1,0:T(8,128)}, u32[]{:S(2)}) copy-start(f32[384,768]{1,0:T(8,128)} %get-tuple-element.5) | copy-start | bytes 3538948
